TPU v7x, 512 devices: a whole 4x8x8 slice. The times are simulated.
512 devices in a mesh: row: 8 (over z), col: 16 (over y_hi, x, core), kpart: 4 (over y_lo).
Axes of the slice: x: 4, y: 8 (y_hi: 2, y_lo: 4; y = y_hi * 4 + y_lo), z: 8, core: 2. Of those that a mesh axis runs over, the one named last changes fastest.
Arguments:
- left_cyclic: float32 [2048, 8192], P(('kpart', 'col'), 'row'), may hold values from -6 to 6
- right_cyclic: float32 [2048, 16384], P(('kpart', 'row'), 'col'), may hold values from -0.125 to 0.125
Outputs:
- product: float32 [8192, 16384], P(('row', 'kpart'), 'col')
All inputs are finite; a program needn't handle non-finite values.
Results may differ from a plain program's by a relative error of at most 0.00007.
Values sent between devices are 32-bit elements; how exact they have to be, the bound alone decides.
No kernel may reach another device: no remote copies, remote signals or barrier semaphores. Data moves between devices by JAX's collectives and lax.ppermute only.
A program may use at most 64 MiB of HBM per device.

v0:
```python
import jax
import jax.numpy as jnp
from jax import lax
from jax.sharding import PartitionSpec as P

NB = 64


def contract(left_part, right_part):
    return lax.dot_general(
        left_part,
        right_part,
        (((0,), (0,)), ((), ())),
        precision=lax.Precision.HIGHEST,
        preferred_element_type=jnp.float32,
    )


def shards(left_cyclic, right_cyclic):
    row_count = lax.axis_size("row")
    column_count = lax.axis_size("col")
    slab_left, local_rows = left_cyclic.shape
    group_left = local_rows // (NB * row_count)
    shaped_left = left_cyclic.reshape(slab_left, row_count, group_left, 1, NB)
    moved_left = lax.all_to_all(shaped_left, "row", split_axis=1, concat_axis=3, tiled=True)
    band_left = moved_left.reshape(slab_left, local_rows)
    left_band = lax.all_gather(band_left, "col", axis=0, tiled=True)
    slab_right, local_cols = right_cyclic.shape
    group_right = local_cols // (NB * column_count)
    shaped_right = right_cyclic.reshape(slab_right, column_count, group_right, 1, NB)
    moved_right = lax.all_to_all(shaped_right, "col", split_axis=1, concat_axis=3, tiled=True)
    band_right = moved_right.reshape(slab_right, local_cols)
    right_band = lax.all_gather(band_right, "row", axis=0, tiled=True)
    return lax.psum_scatter(
        contract(left_band, right_band), "kpart", scatter_dimension=0, tiled=True
    )


def solution(mesh):
    placed = (P(("kpart", "col"), "row"), P(("kpart", "row"), "col"))
    return jax.shard_map(
        shards, mesh=mesh, in_specs=placed, out_specs=P(("row", "kpart"), "col"), check_vma=False
    )
```

profile of v0, /device:TPU:57, one launch (start us, length us, event | category | flops | bytes accessed | tf_op | source)
XLA Modules:
  0.0 246.7 jit_solution(4141008044242358849)
XLA Ops:
  6.5 1.1 reshape.19
  7.6 0.2 copy.11
  7.8 0.3 reshape.23
  8.2 16.5 %all_to_all.24 = f32[16,1,4096]{2,1,0:T(1,128)S(1)} all-to-all(f32[16,1,4096]{2,1,0:T(1,128)S(1)} %reshape.23), channel_id=1, replica_groups=mesh['row'=8,'col'=16,'kpart'=4] {'col'}, dimensions={0} | all-to-all | bytes 524288 | tf_op jit(solution)/shard_map/all_to_all | solution.py:31
  24.7 0.5 broadcast
  25.2 1.2 reduce.1
  26.5 0.2 reshape.24
  26.7 0.3 copy.8
  27.0 0.9 reshape.20
  27.9 0.0 all-gather.5.cloned.1.call-update
  27.9 0.0 all-gather.3.cloned.1.call-start
  28.0 0.2 reshape.17
  28.2 0.1 copy.12
  28.3 0.3 reshape.21
  28.5 17.6 %all_to_all.25 = f32[8,1,4096]{2,1,0:T(1,128)S(1)} all-to-all(f32[8,1,4096]{2,1,0:T(1,128)S(1)} %reshape.21), channel_id=1, replica_groups=mesh['row'=8,'col'=16,'kpart'=4] {'row'}, dimensions={0} | all-to-all | bytes 262144 | tf_op jit(solution)/shard_map/all_to_all | solution.py:25
  46.1 0.9 reduce
  47.1 0.2 reshape.22
  47.3 0.2 copy.6
  47.5 0.8 reshape.18
  48.3 0.0 reduce-scatter.2.cloned.1.call-start
  48.3 25.2 %all-gather.5.cloned.1.call-done = f32[512,1024]{1,0:T(8,128)} async-done(((f32[64,1024]{1,0:T(8,128)}), f32[512,1024]{1,0:T(8,128)}) %all-gather.5.cloned.1.call-update) | async-done | bytes 2097168 | tf_op jit(solution)/shard_map/all_gather | solution.py:33
  73.5 68.3 %all-gather.3.cloned.1.call-done = f32[512,1024]{1,0:T(8,128)} async-done(((f32[32,1024]{1,0:T(8,128)}), f32[512,1024]{1,0:T(8,128)}) %all-gather.3.cloned.1.call-update) | async-done | bytes 2097168 | tf_op jit(solution)/shard_map/all_gather | solution.py:27
  141.8 10.2 %fusion = f32[1024,1024]{1,0:T(8,128)} fusion(f32[512,1024]{1,0:T(8,128)} %all-gather.3.cloned.1.call-done, f32[512,1024]{1,0:T(8,128)} %all-gather.5.cloned.1.call-done), kind=kOutput, calls=%fused_computation.3 | convolution fusion | flops 6442450944 | bytes 8388608 | tf_op jit(solution)/shard_map/dot_general | solution.py:10
  152.0 88.2 %reduce-scatter.2.cloned.1.call-done = f32[256,1024]{1,0:T(8,128)} async-done(((f32[1024,1024]{1,0:T(8,128)}), f32[256,1024]{1,0:T(8,128)}) %reduce-scatter.2.cloned.1.call-update) | async-done | bytes 1048592 | tf_op jit(solution)/shard_map/reduce_scatter | solution.py:34
  (6 shorter events, 0.1 us)
Async XLA Ops:
  6.5 66.9 %all-gather.5.cloned.1.call-start = ((), (), s32[]{:S(2)}) async-start(), calls=%async_computation.4 | async-start | bytes 2359296 | tf_op jit(solution)/shard_map/all_gather | solution.py:33
  8.1 19.8 %copy-start = (f32[32,1024]{1,0:T(8,128)S(1)}, f32[32,1024]{1,0:T(8,128)}, u32[]{:S(2)}) copy-start(f32[32,1024]{1,0:T(8,128)} %param.2) | copy-start | bytes 393220
  27.9 113.9 %all-gather.3.cloned.1.call-start = ((), (), s32[]{:S(2)}) async-start(), calls=%async_computation.3 | async-start | bytes 2228224 | tf_op jit(solution)/shard_map/all_gather | solution.py:27
  48.3 191.9 %reduce-scatter.2.cloned.1.call-start = ((), (), s32[]{:S(2)}) async-start(), calls=%async_computation.5 | async-start | bytes 5242880 | tf_op jit(solution)/shard_map/reduce_scatter | solution.py:34
Sparse Core Ops, SparseCore 0:
  28.0 45.4 all-gather.4
  76.8 64.9 all-gather.2
  152.1 88.0 reduce-scatter.1
where the time goes:
time: 247 us
  waiting for transfers between devices  182 us (74%)
  blocking collectives  34.1 us (14%)
  between operations  13.2 us (5%)
  matrix products  10.2 us (4%)
  local copies, waits for them, and re-layouts  5.21 us (2%)
    reduce_scatter x1, waiting for transfers between devices, shards(): lax.psum_scatter(contract(left_band, right_band), 'kpart', scatter_dimens...  88.2 us
    all_gather x1, waiting for transfers between devices, shards(): left_band = lax.all_gather(band_left, 'col', axis=0, tiled=True)  68.3 us
    all_gather x1, waiting for transfers between devices, shards(): right_band = lax.all_gather(band_right, 'row', axis=0, tiled=True)  25.2 us
    all_to_all x1, blocking collectives, shards(): lax.all_to_all(shaped_left, 'row', split_axis=1, concat_axis=3, tiled=True)  17.6 us
    all_to_all x1, blocking collectives, shards(): lax.all_to_all(shaped_right, 'col', split_axis=1, concat_axis=3, tiled=True)  16.5 us
    dot_general x1, matrix products, contract(): lax.dot_general(left_part, right_part, (((0,), (0,)), ((), ())), precisio...  10.2 us
  transfers between devices with their start and end apart: 3, of which 3 were waited for; matrix products, arithmetic and copies ran while one was open for 1% of the time, Pallas kernels for 0%

commit v1 on v0

--- a/solution.py
+++ b/solution.py
@@ -24,7 +24,8 @@
     shaped_left = left_cyclic.reshape(slab_left, row_count, group_left, 1, NB)
     moved_left = lax.all_to_all(shaped_left, "row", split_axis=1, concat_axis=3, tiled=True)
     band_left = moved_left.reshape(slab_left, local_rows)
-    left_band = lax.all_gather(band_left, "col", axis=0, tiled=True)
+    stack = jnp.stack([band_left] * lax.axis_size("col"))
+    left_band = jnp.concatenate(lax.all_to_all(stack, "col", 0, 0), axis=0)
     slab_right, local_cols = right_cyclic.shape
     group_right = local_cols // (NB * column_count)
     shaped_right = right_cyclic.reshape(slab_right, column_count, group_right, 1, NB)

time: 247 us -> 206 us (0.83)
  waiting for transfers between devices: 182 us -> 141 us
  blocking collectives: 34.1 us -> 0 us
  starting transfers between devices: 0.09 us -> 30.8 us
  local copies, waits for them, and re-layouts: 5.21 us -> 8.43 us
    all_gather x1 -> x0, waiting for transfers between devices: 68.3 us -> none  [shards(): left_band = lax.all_gather(band_left, 'col', axis=0, tiled=True)]
    all_to_all x2 -> x0, blocking collectives: 34.1 us -> none  [the longest x1 17.6 us: shards(): lax.all_to_all(shaped_left, 'row', split_axis=1, concat_axis=3, tiled=True)]
    all_to_all x0 -> x3, starting transfers between devices: none -> 30.8 us  [the longest x1 11.6 us: shards(): lax.all_to_all(shaped_right, 'col', split_axis=1, concat_axis=3, tiled=True)]
    all_gather x1, waiting for transfers between devices: 25.2 us -> 37.9 us  [shards(): right_band = lax.all_gather(band_right, 'row', axis=0, tiled=True)]
    all_to_all x0 -> x3, waiting for transfers between devices: none -> 10.1 us  [the longest x1 5.47 us: shards(): lax.all_to_all(shaped_left, 'row', split_axis=1, concat_axis=3, tiled=True)]
    reduce_scatter x1, waiting for transfers between devices: 88.2 us -> 93.3 us  [shards(): lax.psum_scatter(contract(left_band, right_band), 'kpart', scatter_dimens...]
  transfers between devices with their start and end apart: 3 -> 5, of which waited for: 3 -> 4; matrix products, arithmetic and copies ran while one was open for 1% -> 3% of each run, Pallas kernels for 0% -> 0%
where the time goes in v1:
time: 206 us
  waiting for transfers between devices  141 us (68%)
  starting transfers between devices  30.8 us (15%)
  between operations  13.5 us (7%)
  matrix products  9.5 us (5%)
  local copies, waits for them, and re-layouts  8.43 us (4%)
  other arithmetic  2.16 us (1%)
    reduce_scatter x1, waiting for transfers between devices, shards(): lax.psum_scatter(contract(left_band, right_band), 'kpart', scatter_dimens...  93.3 us
    all_gather x1, waiting for transfers between devices, shards(): right_band = lax.all_gather(band_right, 'row', axis=0, tiled=True)  37.9 us
    all_to_all x1, starting transfers between devices, shards(): lax.all_to_all(shaped_right, 'col', split_axis=1, concat_axis=3, tiled=True)  11.6 us
    all_to_all x1, starting transfers between devices, shards(): lax.all_to_all(shaped_left, 'row', split_axis=1, concat_axis=3, tiled=True)  10 us
    dot_general x1, matrix products, contract(): lax.dot_general(left_part, right_part, (((0,), (0,)), ((), ())), precisio...  9.5 us
    all_to_all x1, starting transfers between devices, shards(): left_band = jnp.concatenate(lax.all_to_all(stack, 'col', 0, 0), axis=0)  9.12 us
    all_to_all x1, waiting for transfers between devices, shards(): lax.all_to_all(shaped_left, 'row', split_axis=1, concat_axis=3, tiled=True)  5.47 us
    all_to_all x1, waiting for transfers between devices, shards(): lax.all_to_all(shaped_right, 'col', split_axis=1, concat_axis=3, tiled=True)  4.58 us
  transfers between devices with their start and end apart: 5, of which 4 were waited for; matrix products, arithmetic and copies ran while one was open for 3% of the time, Pallas kernels for 0%

profile of v1, /device:TPU:57, one launch (start us, length us, event | category | flops | bytes accessed | tf_op | source)
XLA Modules:
  0.0 205.7 jit_solution(1955868504121492220)
XLA Ops:
  6.5 1.1 reshape.19
  7.6 0.1 copy.12
  7.7 0.9 reshape.23
  8.6 10.0 %all-to-all-start = ((f32[8,1,4096]{2,1,0:T(1,128)}), f32[8,1,4096]{2,1,0:T(1,128)S(1)}, u32[]{:S(2)}, u32[]{:S(2)}) async-start(f32[8,1,4096]{2,1,0:T(1,128)} %reshape.23), calls=%async_computation | async-start | bytes 262144 | tf_op jit(solution)/shard_map/all_to_all | solution.py:25
  18.7 1.1 reshape.21
  19.8 0.2 copy.11
  20.0 1.0 reshape.25
  21.0 5.5 %all-to-all-done = f32[8,1,4096]{2,1,0:T(1,128)S(1)} async-done(((f32[8,1,4096]{2,1,0:T(1,128)}), f32[8,1,4096]{2,1,0:T(1,128)S(1)}, u32[]{:S(2)}, u32[]{:S(2)}) %all-to-all-start) | async-done | bytes 131104 | tf_op jit(solution)/shard_map/all_to_all | solution.py:25
  26.5 11.6 %all-to-all-start.2 = ((f32[16,1,4096]{2,1,0:T(1,128)}), f32[16,1,4096]{2,1,0:T(1,128)S(1)}, u32[]{:S(2)}, u32[]{:S(2)}) async-start(f32[16,1,4096]{2,1,0:T(1,128)} %reshape.25), calls=%async_computation.2 | async-start | bytes 524288 | tf_op jit(solution)/shard_map/all_to_all | solution.py:32
  38.1 0.6 broadcast.1
  38.6 0.9 reduce
  39.6 0.2 reshape.24
  39.8 0.2 copy.6
  39.9 0.1 stack_reshape.2
  40.1 4.6 %all-to-all-done.2 = f32[16,1,4096]{2,1,0:T(1,128)S(1)} async-done(((f32[16,1,4096]{2,1,0:T(1,128)}), f32[16,1,4096]{2,1,0:T(1,128)S(1)}, u32[]{:S(2)}, u32[]{:S(2)}) %all-to-all-start.2) | async-done | bytes 262176 | tf_op jit(solution)/shard_map/all_to_all | solution.py:32
  44.7 1.6 stack.3
  46.2 9.1 %all-to-all-start.1 = ((f32[16,32,1024]{2,1,0:T(8,128)}), f32[16,32,1024]{2,1,0:T(8,128)S(1)}, u32[]{:S(2)}, u32[]{:S(2)}) async-start(f32[16,32,1024]{2,1,0:T(8,128)} %stack.3), calls=%async_computation.1 | async-start | bytes 4194304 | tf_op jit(solution)/shard_map/all_to_all | solution.py:28
  55.4 1.2 reduce.1
  56.6 0.2 reshape.26
  56.9 0.3 copy.8
  57.2 0.9 reshape.22
  58.1 37.9 %all-gather.2.cloned.1.call-done = f32[512,1024]{1,0:T(8,128)} async-done(((f32[64,1024]{1,0:T(8,128)}), f32[512,1024]{1,0:T(8,128)}) %all-gather.2.cloned.1.call-update) | async-done | bytes 2097168 | tf_op jit(solution)/shard_map/all_gather | solution.py:34
  96.0 9.5 %fusion = f32[1024,1024]{1,0:T(8,128)} fusion(f32[512,1024]{1,0:T(8,128)S(1)} %bitcast.24, f32[512,1024]{1,0:T(8,128)} %all-gather.2.cloned.1.call-done), kind=kOutput, calls=%fused_computation.3 | convolution fusion | flops 6442450944 | bytes 8388608 | tf_op jit(solution)/shard_map/dot_general | solution.py:10
  105.5 93.3 %reduce-scatter.2.cloned.1.call-done = f32[256,1024]{1,0:T(8,128)} async-done(((f32[1024,1024]{1,0:T(8,128)}), f32[256,1024]{1,0:T(8,128)}) %reduce-scatter.2.cloned.1.call-update) | async-done | bytes 1048592 | tf_op jit(solution)/shard_map/reduce_scatter | solution.py:35
  (6 shorter events, 0.1 us)
Async XLA Ops:
  8.6 17.8 %all-to-all-start = ((f32[8,1,4096]{2,1,0:T(1,128)}), f32[8,1,4096]{2,1,0:T(1,128)S(1)}, u32[]{:S(2)}, u32[]{:S(2)}) async-start(f32[8,1,4096]{2,1,0:T(1,128)} %reshape.23), calls=%async_computation | async-start | bytes 262144 | tf_op jit(solution)/shard_map/all_to_all | solution.py:25
  26.5 18.2 %all-to-all-start.2 = ((f32[16,1,4096]{2,1,0:T(1,128)}), f32[16,1,4096]{2,1,0:T(1,128)S(1)}, u32[]{:S(2)}, u32[]{:S(2)}) async-start(f32[16,1,4096]{2,1,0:T(1,128)} %reshape.25), calls=%async_computation.2 | async-start | bytes 524288 | tf_op jit(solution)/shard_map/all_to_all | solution.py:32
  46.2 49.8 %all-to-all-start.1 = ((f32[16,32,1024]{2,1,0:T(8,128)}), f32[16,32,1024]{2,1,0:T(8,128)S(1)}, u32[]{:S(2)}, u32[]{:S(2)}) async-start(f32[16,32,1024]{2,1,0:T(8,128)} %stack.3), calls=%async_computation.1 | async-start | bytes 4194304 | tf_op jit(solution)/shard_map/all_to_all | solution.py:28
  55.4 40.7 %all-gather.2.cloned.1.call-start = ((), (), s32[]{:S(2)}) async-start(), calls=%async_computation.4 | async-start | bytes 2359296 | tf_op jit(solution)/shard_map/all_gather | solution.py:34
  58.1 140.8 %reduce-scatter.2.cloned.1.call-start = ((), (), s32[]{:S(2)}) async-start(), calls=%async_computation.5 | async-start | bytes 5242880 | tf_op jit(solution)/shard_map/reduce_scatter | solution.py:35
Sparse Core Ops, SparseCore 0:
  58.3 37.6 all-gather.1
  105.7 93.1 reduce-scatter.1
